TPU v7x, 32 devices: a whole 2x2x4 slice. The times are simulated.
32 devices in a mesh: pipe: 4 (over y, core), expert: 4 (over z), dp: 2 (over x).
Axes of the slice: x: 2, y: 2, z: 4, core: 2. Of those that a mesh axis runs over, the one named last changes fastest.
Arguments:
- normed: bfloat16 [4, 4, 384, 4096], P('pipe', None, ('expert', 'dp')), may hold values from -1.5 to 1.5
- saved_out: bfloat16 [4, 4, 384, 2, 4096], P('pipe', None, ('expert', 'dp')), may hold values from -0.59765625 to 0.59765625
- expert_grads: bfloat16 [4, 4, 2, 4, 4, 36, 4096], P('pipe', None, 'dp', 'expert'), may hold values from -24 to 24
- routes: int32 [4, 4, 384, 2], P('pipe', None, ('expert', 'dp')), may hold values from 0 to 3, all different within a row; in each aligned block of 48 rows (0 to 47, 48 to 95, ..., all dimensions but the last counted through in order) at most 36 rows name the same one
- router_weight: bfloat16 [4, 4096, 4], P('pipe'), may hold values from -0.375 to 0.375
- upstream: bfloat16 [4, 384, 4096], P(None, ('expert', 'dp')), may hold values from -6 to 6
Outputs:
- grad_input: bfloat16 [4, 4, 384, 4096], P('pipe', None, ('expert', 'dp'))
- router_grad: float32 [4, 4096, 4], P('pipe')
Inputs may be any that keep to these rules, and one draw needn't show every extreme that they name: `routes`: the two experts of a row differ. Within the 48 rows of one device for one section and micro-batch no expert is named more than 36 times, a bound that some expert reaches in some of these blocks.
All inputs are finite; a program needn't handle non-finite values.
Results may differ from a plain program's by a relative error of at most 0.007.
Values may be sent and summed in bfloat16 or wider, within the bound.
A program may use at most 128 MiB of HBM per device.

v0:
```python
import functools

import jax
import jax.numpy as jnp
from jax import lax
from jax.experimental import pallas as pl
from jax.experimental.pallas import tpu as pltpu
from jax.sharding import PartitionSpec as P

MESH = pl.DeviceIdType.MESH
PACK = 16


def kernel(
    sizes,
    grads_ref,
    tail_ref,
    normed_ref,
    saved_ref,
    upstream_ref,
    routes_ref,
    weight_ref,
    out_ref,
    wgrad_ref,
    main_v,
    tail_v,
    normed_v,
    saved_v,
    inc_v,
    total_v,
    pick_v,
    probs_v,
    chosen_v,
    wpart_v,
    wrecv_v,
    main_send,
    main_recv,
    tail_send,
    tail_recv,
    main_own,
    tail_own,
    load_sem,
    top_sem,
    relay_send,
    relay_recv,
    part_send,
    part_recv,
    sum_send,
    sum_recv,
):
    n_pipe, n_expert, n_dp = sizes
    micro, rows, width = normed_v.shape
    experts = weight_ref.shape[0]
    capacity = grads_ref.shape[2]
    whole_rows = capacity // PACK * PACK
    rest = capacity - whole_rows
    tail_rows = tail_v.shape[1]
    group = n_expert * n_dp
    chunks, _, chunk = wpart_v.shape
    tile = min(width, 512)
    pipe = lax.axis_index("pipe")
    expert = lax.axis_index("expert")
    dp = lax.axis_index("dp")
    me = expert * n_dp + dp

    def member(distance):
        other = lax.rem(me + distance, group)
        return other, {"expert": other // n_dp, "dp": lax.rem(other, n_dp)}

    barrier = pltpu.get_barrier_semaphore()
    for distance in range(1, group):
        _, place = member(distance)
        pl.semaphore_signal(barrier, inc=1, device_id=place, device_id_type=MESH)

    @pl.when(pipe > 0)
    def _():
        pl.semaphore_signal(barrier, inc=1, device_id={"pipe": pipe - 1}, device_id_type=MESH)

    @pl.when(pipe < n_pipe - 1)
    def _():
        pl.semaphore_signal(barrier, inc=1, device_id={"pipe": pipe + 1}, device_id_type=MESH)

    loads = [
        pltpu.make_async_copy(normed_ref, normed_v, load_sem.at[0]),
        pltpu.make_async_copy(saved_ref, saved_v, load_sem.at[1]),
    ]
    top_load = pltpu.make_async_copy(upstream_ref, inc_v, top_sem)
    for load in loads:
        load.start()

    @pl.when(pipe == n_pipe - 1)
    def _():
        top_load.start()

    pl.semaphore_wait(
        barrier,
        group - 1 + jnp.where(pipe > 0, 1, 0) + jnp.where(pipe < n_pipe - 1, 1, 0),
    )

    def tail_copy(distance):
        other = lax.rem(expert + distance, n_expert)
        return pltpu.make_async_remote_copy(
            src_ref=tail_ref.at[other],
            dst_ref=tail_v.at[expert],
            send_sem=tail_send.at[other],
            recv_sem=tail_recv.at[expert],
            device_id={"expert": other},
            device_id_type=MESH,
        )

    def main_copy(m, distance):
        other = lax.rem(expert + distance, n_expert)
        return pltpu.make_async_remote_copy(
            src_ref=grads_ref.at[m, other, pl.ds(0, whole_rows)],
            dst_ref=main_v.at[m, expert],
            send_sem=main_send.at[m, other],
            recv_sem=main_recv.at[m, expert],
            device_id={"expert": other},
            device_id_type=MESH,
        )

    def tail_arrival(distance):
        other = lax.rem(expert + distance, n_expert)
        return pltpu.make_async_remote_copy(
            src_ref=tail_ref.at[other],
            dst_ref=tail_v.at[other],
            send_sem=tail_send.at[other],
            recv_sem=tail_recv.at[other],
            device_id={"expert": other},
            device_id_type=MESH,
        )

    def main_arrival(m, distance):
        other = lax.rem(expert + distance, n_expert)
        return pltpu.make_async_remote_copy(
            src_ref=grads_ref.at[m, other, pl.ds(0, whole_rows)],
            dst_ref=main_v.at[m, other],
            send_sem=main_send.at[m, other],
            recv_sem=main_recv.at[m, other],
            device_id={"expert": other},
            device_id_type=MESH,
        )

    def own_main(m):
        return pltpu.make_async_copy(
            grads_ref.at[m, expert, pl.ds(0, whole_rows)], main_v.at[m, expert], main_own.at[m]
        )

    own_tail = pltpu.make_async_copy(tail_ref.at[expert], tail_v.at[expert], tail_own)

    if rest:
        for distance in range(1, n_expert):
            tail_copy(distance).start()
        own_tail.start()
    if whole_rows:
        for m in range(micro):
            for distance in range(1, n_expert):
                main_copy(m, distance).start()
            own_main(m).start()

    wpart_v[...] = jnp.zeros_like(wpart_v)
    for load in loads:
        load.wait()

    weight = weight_ref[...]
    earlier = (
        lax.broadcasted_iota(jnp.int32, (rows, rows), 0)
        > lax.broadcasted_iota(jnp.int32, (rows, rows), 1)
    ).astype(jnp.bfloat16)
    expert_ids = lax.broadcasted_iota(jnp.int32, (rows, experts), 1)

    def route(m, carry):
        logits = lax.dot_general(
            normed_v[m], weight, (((1,), (1,)), ((), ())), preferred_element_type=jnp.float32
        )
        expl = jnp.exp(logits)
        probs = expl / jnp.sum(expl, axis=-1, keepdims=True)
        probs_v[m] = probs
        named = routes_ref[m]
        first = (named[:, 0:1] == expert_ids).astype(jnp.float32)
        second = (named[:, 1:2] == expert_ids).astype(jnp.float32)
        chosen_v[m, 0] = first
        chosen_v[m, 1] = second
        either = first + second
        before = jnp.dot(earlier, either.astype(jnp.bfloat16), preferred_element_type=jnp.float32)
        slot = jnp.where(either > 0.5, before.astype(jnp.int32), -1)
        parts = []
        if whole_rows:
            ids = lax.broadcasted_iota(jnp.int32, (rows, whole_rows), 1)
            for e in range(experts):
                parts.append(jnp.where(slot[:, e : e + 1] == ids, probs[:, e : e + 1], 0.0))
        if rest:
            ids = lax.broadcasted_iota(jnp.int32, (rows, tail_rows), 1)
            for e in range(experts):
                at = slot[:, e : e + 1]
                there = jnp.where(at >= whole_rows, at - whole_rows + m * rest, -1)
                parts.append(jnp.where(there == ids, probs[:, e : e + 1], 0.0))
        pick = jnp.concatenate(parts, axis=1)
        high = pick.astype(jnp.bfloat16)
        low = (pick - high.astype(jnp.float32)).astype(jnp.bfloat16)
        pick_v[m, pl.ds(0, rows)] = high
        pick_v[m, pl.ds(rows, rows)] = low
        return carry

    lax.fori_loop(0, micro, route, 0)

    if rest:
        for distance in range(1, n_expert):
            tail_arrival(distance).wait_recv()
        own_tail.wait()

    @pl.when(pipe == n_pipe - 1)
    def _():
        top_load.wait()

    main_columns = experts * whole_rows
    pair = lax.broadcasted_iota(jnp.int32, (rows, 2 * rows), 1) - 2 * lax.broadcasted_iota(
        jnp.int32, (rows, 2 * rows), 0
    )

    def relay(m):
        return pltpu.make_async_remote_copy(
            src_ref=out_ref.at[m],
            dst_ref=inc_v.at[m],
            send_sem=relay_send.at[m],
            recv_sem=relay_recv.at[m],
            device_id={"pipe": jnp.maximum(pipe - 1, 0)},
            device_id_type=MESH,
        )

    def block(m, carry):
        if whole_rows:
            for distance in range(1, n_expert):
                main_arrival(m, distance).wait_recv()
            own_main(m).wait()
        pick = pick_v[m]

        def combine(i, inner):
            cols = pl.ds(pl.multiple_of(i * tile, tile), tile)
            both = jnp.zeros((2 * rows, tile), jnp.float32)
            if whole_rows:
                both += jnp.dot(
                    pick[:, :main_columns],
                    main_v[m, :, :, cols].reshape(main_columns, tile),
                    preferred_element_type=jnp.float32,
                )
            if rest:
                both += jnp.dot(
                    pick[:, main_columns:],
                    tail_v[:, :, cols].reshape(experts * tail_rows, tile),
                    preferred_element_type=jnp.float32,
                )
            total_v[:, cols] = both[:rows] + both[rows:]
            return inner

        lax.fori_loop(0, width // tile, combine, 0)

        @pl.when(pipe < n_pipe - 1)
        def _():
            relay(m).wait_recv()

        cross = lax.dot_general(
            inc_v[m], saved_v[m], (((1,), (1,)), ((), ())), preferred_element_type=jnp.float32
        )
        probs = probs_v[m]
        weighted = jnp.zeros((rows, experts), jnp.float32)
        for k in range(2):
            dot = jnp.sum(jnp.where(pair == k, cross, 0.0), axis=1, keepdims=True)
            weighted += dot * probs * chosen_v[m, k]
        dense = (weighted - probs * jnp.sum(weighted, axis=1, keepdims=True)).astype(jnp.bfloat16)

        def finish(i, inner):
            cols = pl.ds(pl.multiple_of(i * tile, tile), tile)
            term = jnp.dot(dense, weight_ref[:, cols], preferred_element_type=jnp.float32)
            whole = inc_v[m, :, cols].astype(jnp.float32) + total_v[:, cols] + term
            out_ref[m, :, cols] = whole.astype(jnp.bfloat16)
            return inner

        lax.fori_loop(0, width // tile, finish, 0)

        @pl.when(pipe > 0)
        def _():
            relay(m).start()

        def weigh(i, inner):
            cols = pl.ds(pl.multiple_of(i * chunk, chunk), chunk)
            wpart_v[i] += lax.dot_general(
                dense,
                normed_v[m, :, cols],
                (((0,), (0,)), ((), ())),
                preferred_element_type=jnp.float32,
            )
            return inner

        lax.fori_loop(0, chunks, weigh, 0)
        return carry

    lax.fori_loop(0, micro, block, 0)

    def part_copy(distance):
        other, place = member(distance)
        return pltpu.make_async_remote_copy(
            src_ref=wpart_v.at[jnp.minimum(other, chunks - 1)],
            dst_ref=wrecv_v.at[me],
            send_sem=part_send.at[other],
            recv_sem=part_recv.at[me],
            device_id=place,
            device_id_type=MESH,
        ), other

    def part_arrival(distance):
        other, place = member(distance)
        return pltpu.make_async_remote_copy(
            src_ref=wpart_v.at[0],
            dst_ref=wrecv_v.at[other],
            send_sem=part_send.at[other],
            recv_sem=part_recv.at[other],
            device_id=place,
            device_id_type=MESH,
        )

    def sum_copy(distance):
        other, place = member(distance)
        spot = jnp.minimum(me, chunks - 1)
        return pltpu.make_async_remote_copy(
            src_ref=wgrad_ref.at[spot],
            dst_ref=wgrad_ref.at[spot],
            send_sem=sum_send.at[other],
            recv_sem=sum_recv.at[me],
            device_id=place,
            device_id_type=MESH,
        )

    def sum_arrival(distance):
        other, place = member(distance)
        spot = jnp.minimum(other, chunks - 1)
        return pltpu.make_async_remote_copy(
            src_ref=wgrad_ref.at[spot],
            dst_ref=wgrad_ref.at[spot],
            send_sem=sum_send.at[other],
            recv_sem=sum_recv.at[other],
            device_id=place,
            device_id_type=MESH,
        ), other

    for distance in range(1, group):
        copy, other = part_copy(distance)

        @pl.when(other < chunks)
        def _():
            copy.start()

    @pl.when(me < chunks)
    def _():
        total = wpart_v[me]
        for distance in range(1, group):
            part_arrival(distance).wait_recv()
            total += wrecv_v[member(distance)[0]]
        wgrad_ref[me] = total * (1.0 / micro)
        for distance in range(1, group):
            sum_copy(distance).start()

    for distance in range(1, group):
        copy, other = sum_arrival(distance)

        @pl.when(other < chunks)
        def _():
            copy.wait_recv()

    if rest:
        for distance in range(1, n_expert):
            tail_copy(distance).wait_send()
    if whole_rows:
        for m in range(micro):
            for distance in range(1, n_expert):
                main_copy(m, distance).wait_send()

    @pl.when(pipe > 0)
    def _():
        for m in range(micro):
            relay(m).wait_send()

    for distance in range(1, group):
        copy, other = part_copy(distance)

        @pl.when(other < chunks)
        def _():
            copy.wait_send()

    @pl.when(me < chunks)
    def _():
        for distance in range(1, group):
            sum_copy(distance).wait_send()


def on_device(sizes, normed, saved_out, expert_grads, routes, router_weight, upstream):
    n_pipe, n_expert, n_dp = sizes
    micro, rows, width = normed.shape[1:]
    experts = router_weight.shape[2]
    capacity = expert_grads.shape[5]
    whole_rows = capacity // PACK * PACK
    rest = capacity - whole_rows
    tail_rows = -(-max(rest * micro, 1) // PACK) * PACK
    group = n_expert * n_dp
    chunks = min(group, width // 128)
    chunk = width // chunks
    grads = expert_grads.reshape(micro, n_expert, capacity, width)
    tail = jnp.transpose(grads[:, :, whole_rows:], (1, 0, 2, 3)).reshape(n_expert, rest * micro, width)
    tail = jnp.pad(tail, ((0, 0), (0, tail_rows - rest * micro), (0, 0)))
    columns = experts * (whole_rows + (tail_rows if rest else 0))
    any_space = pl.BlockSpec(memory_space=pl.ANY)
    vmem = pl.BlockSpec(memory_space=pltpu.VMEM)
    dma = pltpu.SemaphoreType.DMA
    out, wgrad = pl.pallas_call(
        functools.partial(kernel, sizes),
        out_shape=(
            jax.ShapeDtypeStruct((micro, rows, width), jnp.bfloat16),
            jax.ShapeDtypeStruct((chunks, experts, chunk), jnp.float32),
        ),
        in_specs=[any_space] * 5 + [vmem] * 2,
        out_specs=(vmem, vmem),
        scratch_shapes=[
            pltpu.VMEM((micro, n_expert, max(whole_rows, PACK), width), jnp.bfloat16),
            pltpu.VMEM((n_expert, tail_rows, width), jnp.bfloat16),
            pltpu.VMEM((micro, rows, width), jnp.bfloat16),
            pltpu.VMEM((micro, 2 * rows, width), jnp.bfloat16),
            pltpu.VMEM((micro, rows, width), jnp.bfloat16),
            pltpu.VMEM((rows, width), jnp.float32),
            pltpu.VMEM((micro, 2 * rows, columns), jnp.bfloat16),
            pltpu.VMEM((micro, rows, experts), jnp.float32),
            pltpu.VMEM((micro, 2, rows, experts), jnp.float32),
            pltpu.VMEM((chunks, experts, chunk), jnp.float32),
            pltpu.VMEM((group, experts, chunk), jnp.float32),
            dma((micro, n_expert)),
            dma((micro, n_expert)),
            dma((n_expert,)),
            dma((n_expert,)),
            dma((micro,)),
            dma,
            dma((2,)),
            dma,
            dma((micro,)),
            dma((micro,)),
            dma((group,)),
            dma((group,)),
            dma((group,)),
            dma((group,)),
        ],
        compiler_params=pltpu.CompilerParams(
            collective_id=0, has_side_effects=True, vmem_limit_bytes=48 * 2**20
        ),
        name="relay",
    )(
        grads,
        tail,
        normed[0],
        saved_out.reshape(micro, 2 * rows, width),
        upstream,
        routes[0],
        router_weight[0].T,
    )
    router_grad = jnp.transpose(wgrad, (0, 2, 1)).reshape(width, experts)
    return (out[None], router_grad[None])


def solution(mesh):
    in_specs = (
        P("pipe", None, ("expert", "dp"), None),
        P("pipe", None, ("expert", "dp"), None, None),
        P("pipe", None, "dp", "expert", None, None, None),
        P("pipe", None, ("expert", "dp"), None),
        P("pipe", None, None),
        P(None, ("expert", "dp"), None),
    )
    out_specs = (P("pipe", None, ("expert", "dp"), None), P("pipe", None, None))
    sizes = (mesh.shape["pipe"], mesh.shape["expert"], mesh.shape["dp"])
    return jax.shard_map(
        functools.partial(on_device, sizes),
        mesh=mesh,
        in_specs=in_specs,
        out_specs=out_specs,
        check_vma=False,
    )
```

profile of v0, /device:TPU:0, one launch (start us, length us, event | category | flops | bytes accessed | tf_op | source)
XLA Modules:
  0.0 153.4 jit_solution(14359500279632254443)
XLA Ops:
  0.6 0.8 copy.10
  1.4 5.8 %reshape.15.saved_ref = bf16[4,96,4096]{2,1,0:T(8,128)(2,1)} reshape(bf16[1,4,48,2,4096]{4,3,2,1,0:T(2,128)(2,1)} %param.7) | data formatting | bytes 6291456 | tf_op jit(solution)/shard_map/reshape | solution.py:457
  7.2 5.0 %copy.12 = bf16[1,4,1,1,4,36,4096]{6,5,4,1,3,2,0:T(8,128)(2,1)S(1)} copy(bf16[1,4,1,1,4,36,4096]{6,4,5,3,2,1,0:T(4,128)(2,1)} %param.8) | data formatting | bytes 9437184 | tf_op args[2]
  12.2 0.0 copy-start.3
  12.2 0.0 copy-start
  12.2 0.0 copy-start.2
  12.2 0.2 slice_bitcast_fusion
  12.4 2.1 %copy-done.3 = bf16[1,4,1,1,4,36,4096]{6,5,4,1,3,2,0:T(8,128)(2,1)} copy-done((bf16[1,4,1,1,4,36,4096]{6,5,4,1,3,2,0:T(8,128)(2,1)}, bf16[1,4,1,1,4,36,4096]{6,5,4,1,3,2,0:T(8,128)(2,1)S(1)}, u32[]{:S(2)}) %copy-start.3) | copy-done | bytes 4718616
  14.5 0.2 copy.9
  14.7 0.1 reshape.14.tail_ref
  14.8 0.0 copy-done
  14.8 0.0 copy-done.2
  14.8 0.0 copy-start.1
  14.9 1.4 copy-done.1
  16.3 135.3 %relay.1 = (bf16[4,48,4096]{2,1,0:T(8,128)(2,1)S(1)}, f32[8,4,512]{2,1,0:T(4,128)S(1)}) custom-call(bf16[4,4,36,4096]{3,2,1,0:T(8,128)(2,1)} %bitcast.20, bf16[4,16,4096]{2,1,0:T(8,128)(2,1)S(1)} %reshape.14.tail_ref, bf16[4,48,4096]{2,1,0:T(8,128)(2,1)S(1)} %bitcast.14, bf16[4,96,4096]{2,1,0:T(8,128)(2,1)} %reshape.15.saved_ref, ...), custom_call_target="tpu_custom_call" | custom-call | tf_op jit(solution)/shard_map/relay/pallas_call | solution.py:414
  151.6 1.1 copy.15
  152.8 0.6 copy.16
Async XLA Ops:
  12.2 2.3 %copy-start.3 = (bf16[1,4,1,1,4,36,4096]{6,5,4,1,3,2,0:T(8,128)(2,1)}, bf16[1,4,1,1,4,36,4096]{6,5,4,1,3,2,0:T(8,128)(2,1)S(1)}, u32[]{:S(2)}) copy-start(bf16[1,4,1,1,4,36,4096]{6,5,4,1,3,2,0:T(8,128)(2,1)S(1)} %copy.12) | copy-start | bytes 14155780
  12.2 2.7 %copy-start = (bf16[1,4,48,4096]{3,2,1,0:T(8,128)(2,1)S(1)}, bf16[1,4,48,4096]{3,2,1,0:T(8,128)(2,1)}, u32[]{:S(2)}) copy-start(bf16[1,4,48,4096]{3,2,1,0:T(8,128)(2,1)} %param.6) | copy-start | bytes 4718596
  12.2 2.7 %copy-start.2 = (bf16[1,4096,4]{1,2,0:T(4,128)(2,1)S(1)}, bf16[1,4096,4]{1,2,0:T(4,128)(2,1)}, u32[]{:S(2)}) copy-start(bf16[1,4096,4]{1,2,0:T(4,128)(2,1)} %param.10) | copy-start | bytes 98308
  14.8 1.4 copy-start.1
where the time goes:
time: 154 us; the launch traced here: 153 us
  Pallas kernels  135 us (88%)
  local copies, waits for them, and re-layouts  17.3 us (11%)
    pallas_call x1, Pallas kernels, on_device(): pl.pallas_call(functools.partial(kernel, sizes), out_shape=(jax.ShapeDtyp...  135 us
    unnamed x12, local copies, waits for them, and re-layouts  11 us
    reshape x1, local copies, waits for them, and re-layouts, on_device(): saved_out.reshape(micro, 2 * rows, width)  5.76 us

commit v1 on v0

--- a/solution.py
+++ b/solution.py
@@ -25,9 +25,11 @@
     main_v,
     tail_v,
     normed_v,
+    pairs_v,
     saved_v,
     inc_v,
     total_v,
+    dense_v,
     pick_v,
     probs_v,
     chosen_v,
@@ -82,7 +84,7 @@
 
     loads = [
         pltpu.make_async_copy(normed_ref, normed_v, load_sem.at[0]),
-        pltpu.make_async_copy(saved_ref, saved_v, load_sem.at[1]),
+        pltpu.make_async_copy(saved_ref, pairs_v, load_sem.at[1]),
     ]
     top_load = pltpu.make_async_copy(upstream_ref, inc_v, top_sem)
     for load in loads:
@@ -168,6 +170,11 @@
         > lax.broadcasted_iota(jnp.int32, (rows, rows), 1)
     ).astype(jnp.bfloat16)
     expert_ids = lax.broadcasted_iota(jnp.int32, (rows, experts), 1)
+
+    def regroup(i, carry):
+        m, cols = i // (width // tile), pl.ds(pl.multiple_of(lax.rem(i, width // tile) * tile, tile), tile)
+        saved_v[m, :, cols] = pairs_v[m, :, :, cols].reshape(2 * rows, tile)
+        return carry
 
     def route(m, carry):
         logits = lax.dot_general(
@@ -203,6 +210,7 @@
         return carry
 
     lax.fori_loop(0, micro, route, 0)
+    lax.fori_loop(0, micro * (width // tile), regroup, 0)
 
     if rest:
         for distance in range(1, n_expert):
@@ -214,16 +222,17 @@
         top_load.wait()
 
     main_columns = experts * whole_rows
-    pair = lax.broadcasted_iota(jnp.int32, (rows, 2 * rows), 1) - 2 * lax.broadcasted_iota(
-        jnp.int32, (rows, 2 * rows), 0
+    pair = lax.broadcasted_iota(jnp.int32, (PACK, 2 * PACK), 1) - 2 * lax.broadcasted_iota(
+        jnp.int32, (PACK, 2 * PACK), 0
     )
 
-    def relay(m):
-        return pltpu.make_async_remote_copy(
-            src_ref=out_ref.at[m],
-            dst_ref=inc_v.at[m],
-            send_sem=relay_send.at[m],
-            recv_sem=relay_recv.at[m],
+    def relay(m, q):
+        part = pl.ds(pl.multiple_of(q * PACK, PACK), PACK)
+        return pltpu.make_async_remote_copy(
+            src_ref=out_ref.at[m, part],
+            dst_ref=inc_v.at[m, part],
+            send_sem=relay_send.at[m, q],
+            recv_sem=relay_recv.at[m, q],
             device_id={"pipe": jnp.maximum(pipe - 1, 0)},
             device_id_type=MESH,
         )
@@ -255,32 +264,44 @@
 
         lax.fori_loop(0, width // tile, combine, 0)
 
-        @pl.when(pipe < n_pipe - 1)
-        def _():
-            relay(m).wait_recv()
-
-        cross = lax.dot_general(
-            inc_v[m], saved_v[m], (((1,), (1,)), ((), ())), preferred_element_type=jnp.float32
-        )
-        probs = probs_v[m]
-        weighted = jnp.zeros((rows, experts), jnp.float32)
-        for k in range(2):
-            dot = jnp.sum(jnp.where(pair == k, cross, 0.0), axis=1, keepdims=True)
-            weighted += dot * probs * chosen_v[m, k]
-        dense = (weighted - probs * jnp.sum(weighted, axis=1, keepdims=True)).astype(jnp.bfloat16)
-
-        def finish(i, inner):
-            cols = pl.ds(pl.multiple_of(i * tile, tile), tile)
-            term = jnp.dot(dense, weight_ref[:, cols], preferred_element_type=jnp.float32)
-            whole = inc_v[m, :, cols].astype(jnp.float32) + total_v[:, cols] + term
-            out_ref[m, :, cols] = whole.astype(jnp.bfloat16)
+        def step(q, inner):
+            part = pl.ds(pl.multiple_of(q * PACK, PACK), PACK)
+
+            @pl.when(pipe < n_pipe - 1)
+            def _():
+                relay(m, q).wait_recv()
+
+            cross = lax.dot_general(
+                inc_v[m, part],
+                saved_v[m, pl.ds(pl.multiple_of(q * 2 * PACK, 2 * PACK), 2 * PACK)],
+                (((1,), (1,)), ((), ())),
+                preferred_element_type=jnp.float32,
+            )
+            probs = probs_v[m, part]
+            weighted = jnp.zeros((PACK, experts), jnp.float32)
+            for k in range(2):
+                dot = jnp.sum(jnp.where(pair == k, cross, 0.0), axis=1, keepdims=True)
+                weighted += dot * probs * chosen_v[m, k, part]
+            dense = (weighted - probs * jnp.sum(weighted, axis=1, keepdims=True)).astype(jnp.bfloat16)
+            dense_v[part] = dense
+
+            def finish(i, innermost):
+                cols = pl.ds(pl.multiple_of(i * tile, tile), tile)
+                term = jnp.dot(dense, weight_ref[:, cols], preferred_element_type=jnp.float32)
+                whole = inc_v[m, part, cols].astype(jnp.float32) + total_v[part, cols] + term
+                out_ref[m, part, cols] = whole.astype(jnp.bfloat16)
+                return innermost
+
+            lax.fori_loop(0, width // tile, finish, 0, unroll=True)
+
+            @pl.when(pipe > 0)
+            def _():
+                relay(m, q).start()
+
             return inner
 
-        lax.fori_loop(0, width // tile, finish, 0)
-
-        @pl.when(pipe > 0)
-        def _():
-            relay(m).start()
+        lax.fori_loop(0, rows // PACK, step, 0)
+        dense = dense_v[...]
 
         def weigh(i, inner):
             cols = pl.ds(pl.multiple_of(i * chunk, chunk), chunk)
@@ -378,7 +399,8 @@
     @pl.when(pipe > 0)
     def _():
         for m in range(micro):
-            relay(m).wait_send()
+            for q in range(rows // PACK):
+                relay(m, q).wait_send()
 
     for distance in range(1, group):
         copy, other = part_copy(distance)
@@ -423,9 +445,11 @@
             pltpu.VMEM((micro, n_expert, max(whole_rows, PACK), width), jnp.bfloat16),
             pltpu.VMEM((n_expert, tail_rows, width), jnp.bfloat16),
             pltpu.VMEM((micro, rows, width), jnp.bfloat16),
+            pltpu.VMEM((micro, rows, 2, width), jnp.bfloat16),
             pltpu.VMEM((micro, 2 * rows, width), jnp.bfloat16),
             pltpu.VMEM((micro, rows, width), jnp.bfloat16),
             pltpu.VMEM((rows, width), jnp.float32),
+            pltpu.VMEM((rows, experts), jnp.bfloat16),
             pltpu.VMEM((micro, 2 * rows, columns), jnp.bfloat16),
             pltpu.VMEM((micro, rows, experts), jnp.float32),
             pltpu.VMEM((micro, 2, rows, experts), jnp.float32),
@@ -439,22 +463,22 @@
             dma,
             dma((2,)),
             dma,
-            dma((micro,)),
-            dma((micro,)),
+            dma((micro, rows // PACK)),
+            dma((micro, rows // PACK)),
             dma((group,)),
             dma((group,)),
             dma((group,)),
             dma((group,)),
         ],
         compiler_params=pltpu.CompilerParams(
-            collective_id=0, has_side_effects=True, vmem_limit_bytes=48 * 2**20
+            collective_id=0, has_side_effects=True, vmem_limit_bytes=28 * 2**20
         ),
         name="relay",
     )(
         grads,
         tail,
         normed[0],
-        saved_out.reshape(micro, 2 * rows, width),
+        saved_out[0],
         upstream,
         routes[0],
         router_weight[0].T,

time: 154 us -> 152 us (0.987)
  Pallas kernels: 135 us -> 131 us
  local copies, waits for them, and re-layouts: 17.3 us -> 19.7 us
    reshape x1 -> x0, local copies, waits for them, and re-layouts: 5.76 us -> none  [on_device(): saved_out.reshape(micro, 2 * rows, width)]
    unnamed x12 -> x18, local copies, waits for them, and re-layouts: 11 us -> 16.5 us
    pallas_call x1, Pallas kernels: 135 us -> 131 us  [on_device(): pl.pallas_call(functools.partial(kernel, sizes), out_shape=(jax.ShapeDtyp...]
    reshape x1, local copies, waits for them, and re-layouts: 0.12 us -> 1.98 us  [on_device(): jnp.transpose(grads[:, :, whole_rows:], (1, 0, 2, 3))]
where the time goes in v1:
time: 152 us; the launch traced here: 151 us
  Pallas kernels  131 us (86%)
  local copies, waits for them, and re-layouts  19.7 us (13%)
    pallas_call x1, Pallas kernels, on_device(): pl.pallas_call(functools.partial(kernel, sizes), out_shape=(jax.ShapeDtyp...  131 us
    unnamed x18, local copies, waits for them, and re-layouts  16.5 us

profile of v1, /device:TPU:0, one launch (start us, length us, event | category | flops | bytes accessed | tf_op | source)
XLA Modules:
  0.0 151.2 jit_solution(2246070965015207284)
XLA Ops:
  0.6 0.8 copy.10
  1.4 0.0 copy-start.6
  1.4 5.0 %copy.12 = bf16[1,4,1,1,4,36,4096]{6,5,4,1,3,2,0:T(8,128)(2,1)S(1)} copy(bf16[1,4,1,1,4,36,4096]{6,4,5,3,2,1,0:T(4,128)(2,1)} %param.8) | data formatting | bytes 9437184 | tf_op args[2]
  6.4 0.0 copy-start.2
  6.4 0.2 slice_bitcast_fusion
  6.7 0.0 copy-start
  6.7 2.6 %copy-done = bf16[1,4,1,1,4,36,4096]{6,5,4,1,3,2,0:T(8,128)(2,1)} copy-done((bf16[1,4,1,1,4,36,4096]{6,5,4,1,3,2,0:T(8,128)(2,1)}, bf16[1,4,1,1,4,36,4096]{6,5,4,1,3,2,0:T(8,128)(2,1)S(1)}, u32[]{:S(2)}) %copy-start) | copy-done | bytes 4718616
  9.2 1.0 copy.9
  10.2 2.0 %reshape.11.tail_ref = bf16[4,16,4096]{2,1,0:T(8,128)(2,1)} reshape(bf16[4,4,4,4096]{3,2,1,0:T(4,128)(2,1)} %copy.9) | data formatting | bytes 1048576 | tf_op jit(solution)/shard_map/reshape | solution.py:430
  12.2 0.0 copy-done.6
  12.2 0.0 copy-done.2
  12.2 0.0 copy-start.1
  12.2 2.5 %copy-done.1 = bf16[1,4,1,1,4,36,4096]{6,5,4,1,3,2,0:T(8,128)(2,1)S(1)} copy-done((bf16[1,4,1,1,4,36,4096]{6,5,4,1,3,2,0:T(8,128)(2,1)S(1)}, bf16[1,4,1,1,4,36,4096]{6,5,4,1,3,2,0:T(8,128)(2,1)}, u32[]{:S(2)}) %copy-start.1) | copy-done | bytes 4718616
  14.7 0.0 copy-start.3
  14.7 1.0 copy-done.3
  15.8 0.0 copy-start.4
  15.8 1.4 copy-done.4
  17.2 0.0 copy-start.5
  17.2 1.4 copy-done.5
  18.6 130.9 %relay.1 = (bf16[4,48,4096]{2,1,0:T(8,128)(2,1)S(1)}, f32[8,4,512]{2,1,0:T(4,128)S(1)}) custom-call(bf16[4,4,36,4096]{3,2,1,0:T(8,128)(2,1)S(1)} %bitcast.16, bf16[4,16,4096]{2,1,0:T(8,128)(2,1)S(1)} %copy-done.3, bf16[4,48,4096]{2,1,0:T(8,128)(2,1)S(1)} %bitcast.18, bf16[4,48,2,4096]{3,2,1,0:T(2,128)(2,1)S(1)} %bitcast.17, ...), custom_call_target="tpu_custom_call" | custom-call | tf_op jit(solution)/shard_map/relay/pallas_call | solution.py:436
  149.5 1.1 copy.15
  150.6 0.6 copy.16
Async XLA Ops:
  1.4 10.8 %copy-start.6 = (bf16[1,4096,4]{1,2,0:T(4,128)(2,1)S(1)}, bf16[1,4096,4]{1,2,0:T(4,128)(2,1)}, u32[]{:S(2)}) copy-start(bf16[1,4096,4]{1,2,0:T(4,128)(2,1)} %param.10) | copy-start | bytes 98308
  6.4 5.8 %copy-start.2 = (bf16[1,4,48,2,4096]{4,3,2,1,0:T(2,128)(2,1)S(1)}, bf16[1,4,48,2,4096]{4,3,2,1,0:T(2,128)(2,1)}, u32[]{:S(2)}) copy-start(bf16[1,4,48,2,4096]{4,3,2,1,0:T(2,128)(2,1)} %param.7) | copy-start | bytes 9437188
  6.7 2.6 %copy-start = (bf16[1,4,1,1,4,36,4096]{6,5,4,1,3,2,0:T(8,128)(2,1)}, bf16[1,4,1,1,4,36,4096]{6,5,4,1,3,2,0:T(8,128)(2,1)S(1)}, u32[]{:S(2)}) copy-start(bf16[1,4,1,1,4,36,4096]{6,5,4,1,3,2,0:T(8,128)(2,1)S(1)} %copy.12) | copy-start | bytes 14155780
  12.2 2.5 %copy-start.1 = (bf16[1,4,1,1,4,36,4096]{6,5,4,1,3,2,0:T(8,128)(2,1)S(1)}, bf16[1,4,1,1,4,36,4096]{6,5,4,1,3,2,0:T(8,128)(2,1)}, u32[]{:S(2)}) copy-start(bf16[1,4,1,1,4,36,4096]{6,5,4,1,3,2,0:T(8,128)(2,1)} %copy-done) | copy-start | bytes 14155780
  14.7 1.0 copy-start.3
  15.8 1.4 copy-start.4
  17.2 1.4 copy-start.5

commit v2 on v1

--- a/solution.py
+++ b/solution.py
@@ -14,7 +14,6 @@
 def kernel(
     sizes,
     grads_ref,
-    tail_ref,
     normed_ref,
     saved_ref,
     upstream_ref,
@@ -22,8 +21,13 @@
     weight_ref,
     out_ref,
     wgrad_ref,
+    grads_v,
     main_v,
     tail_v,
+    mate_main_v,
+    mate_tail_v,
+    sums_v,
+    terms_v,
     normed_v,
     pairs_v,
     saved_v,
@@ -31,16 +35,20 @@
     total_v,
     dense_v,
     pick_v,
+    asked_v,
     probs_v,
     chosen_v,
     wpart_v,
     wrecv_v,
+    grads_sem,
     main_send,
     main_recv,
     tail_send,
     tail_recv,
-    main_own,
-    tail_own,
+    pick_send,
+    pick_recv,
+    term_send,
+    term_recv,
     load_sem,
     top_sem,
     relay_send,
@@ -53,10 +61,12 @@
     n_pipe, n_expert, n_dp = sizes
     micro, rows, width = normed_v.shape
     experts = weight_ref.shape[0]
-    capacity = grads_ref.shape[2]
+    capacity = grads_ref.shape[1]
     whole_rows = capacity // PACK * PACK
     rest = capacity - whole_rows
     tail_rows = tail_v.shape[1]
+    columns = pick_v.shape[3]
+    n_pairs = n_expert // 2
     group = n_expert * n_dp
     chunks, _, chunk = wpart_v.shape
     tile = min(width, 512)
@@ -64,6 +74,12 @@
     expert = lax.axis_index("expert")
     dp = lax.axis_index("dp")
     me = expert * n_dp + dp
+    pair = expert // 2
+    odd = lax.rem(expert, 2)
+    mate = expert + 1 - 2 * odd
+
+    def summed_here(j):
+        return ((odd == 1) & (j > expert)) | ((odd == 0) & (j < expert))
 
     def member(distance):
         other = lax.rem(me + distance, group)
@@ -82,6 +98,11 @@
     def _():
         pl.semaphore_signal(barrier, inc=1, device_id={"pipe": pipe + 1}, device_id_type=MESH)
 
+    def grads_load(m):
+        return pltpu.make_async_copy(grads_ref.at[m], grads_v.at[m], grads_sem.at[m])
+
+    for m in range(micro):
+        grads_load(m).start()
     loads = [
         pltpu.make_async_copy(normed_ref, normed_v, load_sem.at[0]),
         pltpu.make_async_copy(saved_ref, pairs_v, load_sem.at[1]),
@@ -99,66 +120,131 @@
         group - 1 + jnp.where(pipe > 0, 1, 0) + jnp.where(pipe < n_pipe - 1, 1, 0),
     )
 
-    def tail_copy(distance):
-        other = lax.rem(expert + distance, n_expert)
-        return pltpu.make_async_remote_copy(
-            src_ref=tail_ref.at[other],
-            dst_ref=tail_v.at[expert],
-            send_sem=tail_send.at[other],
-            recv_sem=tail_recv.at[expert],
-            device_id={"expert": other},
-            device_id_type=MESH,
-        )
-
-    def main_copy(m, distance):
-        other = lax.rem(expert + distance, n_expert)
-        return pltpu.make_async_remote_copy(
-            src_ref=grads_ref.at[m, other, pl.ds(0, whole_rows)],
-            dst_ref=main_v.at[m, expert],
-            send_sem=main_send.at[m, other],
-            recv_sem=main_recv.at[m, expert],
-            device_id={"expert": other},
-            device_id_type=MESH,
-        )
-
-    def tail_arrival(distance):
-        other = lax.rem(expert + distance, n_expert)
-        return pltpu.make_async_remote_copy(
-            src_ref=tail_ref.at[other],
-            dst_ref=tail_v.at[other],
-            send_sem=tail_send.at[other],
-            recv_sem=tail_recv.at[other],
-            device_id={"expert": other},
-            device_id_type=MESH,
-        )
-
-    def main_arrival(m, distance):
-        other = lax.rem(expert + distance, n_expert)
-        return pltpu.make_async_remote_copy(
-            src_ref=grads_ref.at[m, other, pl.ds(0, whole_rows)],
-            dst_ref=main_v.at[m, other],
-            send_sem=main_send.at[m, other],
-            recv_sem=main_recv.at[m, other],
-            device_id={"expert": other},
-            device_id_type=MESH,
-        )
-
-    def own_main(m):
-        return pltpu.make_async_copy(
-            grads_ref.at[m, expert, pl.ds(0, whole_rows)], main_v.at[m, expert], main_own.at[m]
-        )
-
-    own_tail = pltpu.make_async_copy(tail_ref.at[expert], tail_v.at[expert], tail_own)
+    def tail_copy(j):
+        return pltpu.make_async_remote_copy(
+            src_ref=tail_v.at[j],
+            dst_ref=mate_tail_v.at[j],
+            send_sem=tail_send.at[j],
+            recv_sem=tail_recv.at[j],
+            device_id={"expert": mate},
+            device_id_type=MESH,
+        )
+
+    def main_copy(m, j):
+        return pltpu.make_async_remote_copy(
+            src_ref=main_v.at[m, j],
+            dst_ref=mate_main_v.at[m, j],
+            send_sem=main_send.at[m, j],
+            recv_sem=main_recv.at[m, j],
+            device_id={"expert": mate},
+            device_id_type=MESH,
+        )
+
+    def first_of(p):
+        return jnp.where(p == pair, expert, jnp.where(p < pair, 2 * p + 1, 2 * p))
+
+    def pick_copy(p):
+        return pltpu.make_async_remote_copy(
+            src_ref=pick_v.at[p],
+            dst_ref=asked_v.at[expert],
+            send_sem=pick_send.at[p],
+            recv_sem=pick_recv.at[expert],
+            device_id={"expert": first_of(p)},
+            device_id_type=MESH,
+        )
+
+    def pick_arrival(j):
+        return pltpu.make_async_remote_copy(
+            src_ref=pick_v.at[0],
+            dst_ref=asked_v.at[j],
+            send_sem=pick_send.at[0],
+            recv_sem=pick_recv.at[j],
+            device_id={"expert": j},
+            device_id_type=MESH,
+        )
+
+    def term_copy(m, j):
+        return pltpu.make_async_remote_copy(
+            src_ref=sums_v.at[lax.rem(m, 2), j],
+            dst_ref=terms_v.at[m, pair],
+            send_sem=term_send.at[m, j],
+            recv_sem=term_recv.at[m, pair],
+            device_id={"expert": j},
+            device_id_type=MESH,
+        )
+
+    def term_arrival(m, p):
+        return pltpu.make_async_remote_copy(
+            src_ref=sums_v.at[0, 0],
+            dst_ref=terms_v.at[m, p],
+            send_sem=term_send.at[m, 0],
+            recv_sem=term_recv.at[m, p],
+            device_id={"expert": first_of(p)},
+            device_id_type=MESH,
+        )
+
+    def far(t):
+        j = jnp.where(odd == 1, t, n_expert - 1 - t)
+        return j, (j != expert) & (j != mate) & jnp.logical_not(summed_here(j))
+
+    tiles = width // tile
+
+    def columns_of(i):
+        return pl.ds(pl.multiple_of(i * tile, tile), tile)
 
     if rest:
-        for distance in range(1, n_expert):
-            tail_copy(distance).start()
-        own_tail.start()
+        shape = (n_expert * tail_rows, micro * rest * n_expert)
+        row, col = (lax.broadcasted_iota(jnp.int32, shape, axis) for axis in (0, 1))
+        tail_order = (
+            col == lax.rem(row, tail_rows) * n_expert + lax.div(row, tail_rows)
+        ).astype(jnp.bfloat16)
     if whole_rows:
-        for m in range(micro):
-            for distance in range(1, n_expert):
-                main_copy(m, distance).start()
-            own_main(m).start()
+        shape = (n_expert * whole_rows, n_expert * whole_rows)
+        row, col = (lax.broadcasted_iota(jnp.int32, shape, axis) for axis in (0, 1))
+        main_order = (
+            col == lax.rem(row, whole_rows) * n_expert + lax.div(row, whole_rows)
+        ).astype(jnp.bfloat16)
+
+    def regroup_tail(i, carry):
+        cols = columns_of(i)
+        slots = jnp.concatenate(
+            [
+                grads_v[m, whole_rows:, :, cols].reshape(rest * n_expert, tile)
+                for m in range(micro)
+            ],
+            axis=0,
+        )
+        ordered = jnp.dot(tail_order, slots, preferred_element_type=jnp.float32)
+        tail_v[:, :, cols] = ordered.astype(jnp.bfloat16).reshape(n_expert, tail_rows, tile)
+        return carry
+
+    def regroup_main(m):
+        def regroup(i, carry):
+            cols = columns_of(i)
+            slots = grads_v[m, :whole_rows, :, cols].reshape(whole_rows * n_expert, tile)
+            ordered = jnp.dot(main_order, slots, preferred_element_type=jnp.float32)
+            main_v[m, :, :, cols] = ordered.astype(jnp.bfloat16).reshape(
+                n_expert, whole_rows, tile
+            )
+            return carry
+
+        lax.fori_loop(0, tiles, regroup, 0)
+
+    for m in range(micro):
+        grads_load(m).wait()
+    if rest:
+        lax.fori_loop(0, tiles, regroup_tail, 0)
+    if whole_rows:
+        regroup_main(0)
+    for t in range(n_expert):
+        j, send = far(t)
+
+        @pl.when(send)
+        def _():
+            if rest:
+                tail_copy(j).start()
+            if whole_rows:
+                main_copy(0, j).start()
 
     wpart_v[...] = jnp.zeros_like(wpart_v)
     for load in loads:
@@ -191,38 +277,109 @@
         either = first + second
         before = jnp.dot(earlier, either.astype(jnp.bfloat16), preferred_element_type=jnp.float32)
         slot = jnp.where(either > 0.5, before.astype(jnp.int32), -1)
-        parts = []
+        ids = lax.broadcasted_iota(jnp.int32, (rows, columns), 1)
+        for p in range(n_pairs):
+            first_expert = first_of(p)
+            pick = jnp.zeros((rows, columns), jnp.float32)
+            for place, e in enumerate((first_expert, 4 * p + 1 - first_expert)):
+                this = expert_ids == e
+                at = jnp.sum(jnp.where(this, slot, 0), axis=1, keepdims=True)
+                gate = jnp.sum(jnp.where(this, probs, 0.0), axis=1, keepdims=True)
+                late = 2 * whole_rows + place * tail_rows + at - whole_rows + m * rest
+                there = jnp.where(at < whole_rows, at + place * whole_rows, late)
+                there = jnp.where(at < 0, -1, there)
+                pick += jnp.where(there == ids, gate, 0.0)
+            high = pick.astype(jnp.bfloat16)
+            low = (pick - high.astype(jnp.float32)).astype(jnp.bfloat16)
+            pick_v[p, m, pl.ds(0, rows)] = high
+            pick_v[p, m, pl.ds(rows, rows)] = low
+        return carry
+
+    lax.fori_loop(0, micro, route, 0)
+    for p in range(n_pairs):
+
+        @pl.when(p != pair)
+        def _():
+            pick_copy(p).start()
+
+    def send_near(m):
+        if rest and m == 0:
+            tail_copy(mate).start()
         if whole_rows:
-            ids = lax.broadcasted_iota(jnp.int32, (rows, whole_rows), 1)
-            for e in range(experts):
-                parts.append(jnp.where(slot[:, e : e + 1] == ids, probs[:, e : e + 1], 0.0))
-        if rest:
-            ids = lax.broadcasted_iota(jnp.int32, (rows, tail_rows), 1)
-            for e in range(experts):
-                at = slot[:, e : e + 1]
-                there = jnp.where(at >= whole_rows, at - whole_rows + m * rest, -1)
-                parts.append(jnp.where(there == ids, probs[:, e : e + 1], 0.0))
-        pick = jnp.concatenate(parts, axis=1)
-        high = pick.astype(jnp.bfloat16)
-        low = (pick - high.astype(jnp.float32)).astype(jnp.bfloat16)
-        pick_v[m, pl.ds(0, rows)] = high
-        pick_v[m, pl.ds(rows, rows)] = low
-        return carry
-
-    lax.fori_loop(0, micro, route, 0)
+            main_copy(m, mate).start()
+
+    for m in range(1, micro):
+        if whole_rows:
+            regroup_main(m)
+            for t in range(n_expert):
+                j, send = far(t)
+
+                @pl.when(send)
+                def _():
+                    main_copy(m, j).start()
+
+        send_near(m - 1)
+    send_near(micro - 1)
+
     lax.fori_loop(0, micro * (width // tile), regroup, 0)
-
-    if rest:
-        for distance in range(1, n_expert):
-            tail_arrival(distance).wait_recv()
-        own_tail.wait()
 
     @pl.when(pipe == n_pipe - 1)
     def _():
         top_load.wait()
 
-    main_columns = experts * whole_rows
-    pair = lax.broadcasted_iota(jnp.int32, (PACK, 2 * PACK), 1) - 2 * lax.broadcasted_iota(
+    def await_slots(m, j):
+        if whole_rows:
+            main_copy(m, j).wait_recv()
+        if rest:
+
+            @pl.when(m == 0)
+            def _():
+                tail_copy(j).wait_recv()
+
+    def picked(m, j, pick, cols):
+        slots = []
+        if whole_rows:
+            slots += [main_v[m, j, :, cols], mate_main_v[m, j, :, cols]]
+        if rest:
+            slots += [tail_v[j, :, cols], mate_tail_v[j, :, cols]]
+        both = jnp.dot(
+            pick, jnp.concatenate(slots, axis=0), preferred_element_type=jnp.float32
+        )
+        return both[:rows] + both[rows:]
+
+    def sum_for_others(m):
+        def one(t, carry):
+            j = jnp.where(odd == 1, n_expert - 1 - t, t)
+
+            @pl.when(summed_here(j))
+            def _():
+                await_slots(m, j)
+
+                @pl.when(m == 0)
+                def _():
+                    pick_arrival(j).wait_recv()
+
+                @pl.when(m >= 2)
+                def _():
+                    term_copy(m - 2, j).wait_send()
+
+                pick = asked_v[j, m]
+
+                def combine(i, inner):
+                    cols = columns_of(i)
+                    sums_v[lax.rem(m, 2), j, :, cols] = picked(m, j, pick, cols).astype(
+                        jnp.bfloat16
+                    )
+                    return inner
+
+                lax.fori_loop(0, tiles, combine, 0)
+                term_copy(m, j).start()
+
+            return carry
+
+        lax.fori_loop(0, n_expert, one, 0)
+
+    offset = lax.broadcasted_iota(jnp.int32, (PACK, 2 * PACK), 1) - 2 * lax.broadcasted_iota(
         jnp.int32, (PACK, 2 * PACK), 0
     )
 
@@ -237,32 +394,32 @@
             device_id_type=MESH,
         )
 
-    def block(m, carry):
-        if whole_rows:
-            for distance in range(1, n_expert):
-                main_arrival(m, distance).wait_recv()
-            own_main(m).wait()
-        pick = pick_v[m]
+    def block(m):
+        await_slots(m, expert)
+        pick = pick_v[pair, m]
 
         def combine(i, inner):
-            cols = pl.ds(pl.multiple_of(i * tile, tile), tile)
-            both = jnp.zeros((2 * rows, tile), jnp.float32)
-            if whole_rows:
-                both += jnp.dot(
-                    pick[:, :main_columns],
-                    main_v[m, :, :, cols].reshape(main_columns, tile),
-                    preferred_element_type=jnp.float32,
-                )
-            if rest:
-                both += jnp.dot(
-                    pick[:, main_columns:],
-                    tail_v[:, :, cols].reshape(experts * tail_rows, tile),
-                    preferred_element_type=jnp.float32,
-                )
-            total_v[:, cols] = both[:rows] + both[rows:]
+            cols = columns_of(i)
+            total_v[:, cols] = picked(m, expert, pick, cols)
             return inner
 
-        lax.fori_loop(0, width // tile, combine, 0)
+        lax.fori_loop(0, tiles, combine, 0)
+
+        def join(p, carry):
+            @pl.when(p != pair)
+            def _():
+                term_arrival(m, p).wait_recv()
+
+                def add(i, inner):
+                    cols = columns_of(i)
+                    total_v[:, cols] += terms_v[m, p, :, cols].astype(jnp.float32)
+                    return inner
+
+                lax.fori_loop(0, tiles, add, 0)
+
+            return carry
+
+        lax.fori_loop(0, n_pairs, join, 0)
 
         def step(q, inner):
             part = pl.ds(pl.multiple_of(q * PACK, PACK), PACK)
@@ -280,7 +437,7 @@
             probs = probs_v[m, part]
             weighted = jnp.zeros((PACK, experts), jnp.float32)
             for k in range(2):
-                dot = jnp.sum(jnp.where(pair == k, cross, 0.0), axis=1, keepdims=True)
+                dot = jnp.sum(jnp.where(offset == k, cross, 0.0), axis=1, keepdims=True)
                 weighted += dot * probs * chosen_v[m, k, part]
             dense = (weighted - probs * jnp.sum(weighted, axis=1, keepdims=True)).astype(jnp.bfloat16)
             dense_v[part] = dense
@@ -314,9 +471,19 @@
             return inner
 
         lax.fori_loop(0, chunks, weigh, 0)
+
+    def turn(m, carry):
+        @pl.when(m < micro)
+        def _():
+            sum_for_others(m)
+
+        @pl.when(m > 0)
+        def _():
+            block(m - 1)
+
         return carry
 
-    lax.fori_loop(0, micro, block, 0)
+    lax.fori_loop(0, micro + 1, turn, 0)
 
     def part_copy(distance):
         other, place = member(distance)
@@ -388,13 +555,26 @@
         def _():
             copy.wait_recv()
 
-    if rest:
-        for distance in range(1, n_expert):
-            tail_copy(distance).wait_send()
-    if whole_rows:
-        for m in range(micro):
-            for distance in range(1, n_expert):
-                main_copy(m, distance).wait_send()
+    for j in range(n_expert):
+
+        @pl.when((expert != j) & jnp.logical_not(summed_here(j)))
+        def _():
+            if rest:
+                tail_copy(j).wait_send()
+            if whole_rows:
+                for m in range(micro):
+                    main_copy(m, j).wait_send()
+
+        @pl.when(summed_here(j))
+        def _():
+            for m in range(max(micro - 2, 0), micro):
+                term_copy(m, j).wait_send()
+
+    for p in range(n_pairs):
+
+        @pl.when(p != pair)
+        def _():
+            pick_copy(p).wait_send()
 
     @pl.when(pipe > 0)
     def _():
@@ -426,10 +606,13 @@
     group = n_expert * n_dp
     chunks = min(group, width // 128)
     chunk = width // chunks
-    grads = expert_grads.reshape(micro, n_expert, capacity, width)
-    tail = jnp.transpose(grads[:, :, whole_rows:], (1, 0, 2, 3)).reshape(n_expert, rest * micro, width)
-    tail = jnp.pad(tail, ((0, 0), (0, tail_rows - rest * micro), (0, 0)))
-    columns = experts * (whole_rows + (tail_rows if rest else 0))
+    grads = jnp.swapaxes(expert_grads.reshape(micro, n_expert, capacity, width), 1, 2)
+    columns = 2 * (whole_rows + (tail_rows if rest else 0))
+    main_shape = (
+        (micro, n_expert, whole_rows, width) if whole_rows else (1, 1, PACK, width)
+    )
+    tail_shape = (n_expert, tail_rows, width) if rest else (1, tail_rows, width)
+    n_pairs = n_expert // 2
     any_space = pl.BlockSpec(memory_space=pl.ANY)
     vmem = pl.BlockSpec(memory_space=pltpu.VMEM)
     dma = pltpu.SemaphoreType.DMA
@@ -439,28 +622,37 @@
             jax.ShapeDtypeStruct((micro, rows, width), jnp.bfloat16),
             jax.ShapeDtypeStruct((chunks, experts, chunk), jnp.float32),
         ),
-        in_specs=[any_space] * 5 + [vmem] * 2,
+        in_specs=[any_space] * 4 + [vmem] * 2,
         out_specs=(vmem, vmem),
         scratch_shapes=[
-            pltpu.VMEM((micro, n_expert, max(whole_rows, PACK), width), jnp.bfloat16),
-            pltpu.VMEM((n_expert, tail_rows, width), jnp.bfloat16),
+            pltpu.VMEM((micro, capacity, n_expert, width), jnp.bfloat16),
+            pltpu.VMEM(main_shape, jnp.bfloat16),
+            pltpu.VMEM(tail_shape, jnp.bfloat16),
+            pltpu.VMEM(main_shape, jnp.bfloat16),
+            pltpu.VMEM(tail_shape, jnp.bfloat16),
+            pltpu.VMEM((2, n_expert, rows, width), jnp.bfloat16),
+            pltpu.VMEM((micro, n_pairs, rows, width), jnp.bfloat16),
             pltpu.VMEM((micro, rows, width), jnp.bfloat16),
             pltpu.VMEM((micro, rows, 2, width), jnp.bfloat16),
             pltpu.VMEM((micro, 2 * rows, width), jnp.bfloat16),
             pltpu.VMEM((micro, rows, width), jnp.bfloat16),
             pltpu.VMEM((rows, width), jnp.float32),
             pltpu.VMEM((rows, experts), jnp.bfloat16),
-            pltpu.VMEM((micro, 2 * rows, columns), jnp.bfloat16),
+            pltpu.VMEM((n_pairs, micro, 2 * rows, columns), jnp.bfloat16),
+            pltpu.VMEM((n_expert, micro, 2 * rows, columns), jnp.bfloat16),
             pltpu.VMEM((micro, rows, experts), jnp.float32),
             pltpu.VMEM((micro, 2, rows, experts), jnp.float32),
             pltpu.VMEM((chunks, experts, chunk), jnp.float32),
             pltpu.VMEM((group, experts, chunk), jnp.float32),
+            dma((micro,)),
             dma((micro, n_expert)),
             dma((micro, n_expert)),
             dma((n_expert,)),
             dma((n_expert,)),
-            dma((micro,)),
-            dma,
+            dma((n_pairs,)),
+            dma((n_expert,)),
+            dma((micro, n_expert)),
+            dma((micro, n_pairs)),
             dma((2,)),
             dma,
             dma((micro, rows // PACK)),
@@ -471,12 +663,11 @@
             dma((group,)),
         ],
         compiler_params=pltpu.CompilerParams(
-            collective_id=0, has_side_effects=True, vmem_limit_bytes=28 * 2**20
+            collective_id=0, has_side_effects=True, vmem_limit_bytes=60 * 2**20
         ),
         name="relay",
     )(
         grads,
-        tail,
         normed[0],
         saved_out[0],
         upstream,

time: 152 us -> 128 us (0.84)
  local copies, waits for them, and re-layouts: 19.7 us -> 4.8 us
  Pallas kernels: 131 us -> 122 us
    unnamed x18 -> x5, local copies, waits for them, and re-layouts: 16.5 us -> 4.8 us
    pallas_call x1, Pallas kernels: 131 us -> 122 us  [on_device(): pl.pallas_call(functools.partial(kernel, sizes), out_shape=(jax.ShapeDtyp...]
    reshape x1 -> x0, local copies, waits for them, and re-layouts: 1.98 us -> none  [on_device(): jnp.transpose(grads[:, :, whole_rows:], (1, 0, 2, 3))]
where the time goes in v2:
time: 128 us
  Pallas kernels  122 us (95%)
  local copies, waits for them, and re-layouts  4.8 us (4%)
    pallas_call x1, Pallas kernels, on_device(): pl.pallas_call(functools.partial(kernel, sizes), out_shape=(jax.ShapeDtyp...  122 us
    unnamed x5, local copies, waits for them, and re-layouts  4.8 us

profile of v2, /device:TPU:0, one launch (start us, length us, event | category | flops | bytes accessed | tf_op | source)
XLA Modules:
  0.0 127.9 jit_solution(4423768701598208919)
XLA Ops:
  0.6 1.4 %copy.8 = s32[1,4,48,2]{3,2,1,0:T(8,128)} copy(s32[1,4,48,2]{2,3,1,0:T(2,128)} %param.9) | data formatting | bytes 3072 | tf_op args[3]
  2.1 122.5 %relay.1 = (bf16[4,48,4096]{2,1,0:T(8,128)(2,1)}, f32[8,4,512]{2,1,0:T(4,128)}) custom-call(bf16[4,36,4,4096]{3,2,1,0:T(4,128)(2,1)} %bitcast.13, bf16[4,48,4096]{2,1,0:T(8,128)(2,1)} %bitcast.16, bf16[4,48,2,4096]{3,2,1,0:T(2,128)(2,1)} %bitcast.14, bf16[4,48,4096]{2,1,0:T(8,128)(2,1)} %upstream_ref.1, s32[4,48,2]{2,1,0:T(8,128)} %bitcast.17, ...), custom_call_target="tpu_custom_call" | custom-call | tf_op jit(solution)/shard_map/relay/pallas_call | solution.py:619
  124.5 0.0 copy-start
  124.5 2.7 %copy.11 = bf16[1,4,48,4096]{3,2,1,0:T(8,128)(2,1)} copy(bf16[1,4,48,4096]{3,2,1,0:T(8,128)(2,1)} %bitcast.15) | data formatting | bytes 3145728
  127.3 0.0 copy-done
  127.3 0.6 copy.12
Async XLA Ops:
  124.5 2.7 %copy-start = (f32[8,4,512]{2,1,0:T(4,128)S(1)}, f32[8,4,512]{2,1,0:T(4,128)}, u32[]{:S(2)}) copy-start(f32[8,4,512]{2,1,0:T(4,128)} %get-tuple-element.5) | copy-start | bytes 196612

commit v3 on v2

--- a/solution.py
+++ b/solution.py
@@ -145,7 +145,7 @@
 
     def pick_copy(p):
         return pltpu.make_async_remote_copy(
-            src_ref=pick_v.at[p],
+            src_ref=pick_v.at[p, :, pl.ds(0, rows)],
             dst_ref=asked_v.at[expert],
             send_sem=pick_send.at[p],
             recv_sem=pick_recv.at[expert],
@@ -155,7 +155,7 @@
 
     def pick_arrival(j):
         return pltpu.make_async_remote_copy(
-            src_ref=pick_v.at[0],
+            src_ref=pick_v.at[0, :, pl.ds(0, rows)],
             dst_ref=asked_v.at[j],
             send_sem=pick_send.at[0],
             recv_sem=pick_recv.at[j],
@@ -228,15 +228,9 @@
             )
             return carry
 
-        lax.fori_loop(0, tiles, regroup, 0)
-
-    for m in range(micro):
-        grads_load(m).wait()
-    if rest:
-        lax.fori_loop(0, tiles, regroup_tail, 0)
-    if whole_rows:
-        regroup_main(0)
-    for t in range(n_expert):
+        lax.fori_loop(0, tiles, regroup, 0, unroll=4)
+
+    def send_first(t):
         j, send = far(t)
 
         @pl.when(send)
@@ -245,6 +239,14 @@
                 tail_copy(j).start()
             if whole_rows:
                 main_copy(0, j).start()
+
+    for m in range(micro):
+        grads_load(m).wait()
+    if rest:
+        lax.fori_loop(0, tiles, regroup_tail, 0, unroll=4)
+    if whole_rows:
+        regroup_main(0)
+    send_first(0)
 
     wpart_v[...] = jnp.zeros_like(wpart_v)
     for load in loads:
@@ -302,6 +304,9 @@
         def _():
             pick_copy(p).start()
 
+    for t in range(1, n_expert):
+        send_first(t)
+
     def send_near(m):
         if rest and m == 0:
             tail_copy(mate).start()
@@ -342,10 +347,9 @@
             slots += [main_v[m, j, :, cols], mate_main_v[m, j, :, cols]]
         if rest:
             slots += [tail_v[j, :, cols], mate_tail_v[j, :, cols]]
-        both = jnp.dot(
+        return jnp.dot(
             pick, jnp.concatenate(slots, axis=0), preferred_element_type=jnp.float32
         )
-        return both[:rows] + both[rows:]
 
     def sum_for_others(m):
         def one(t, carry):
@@ -372,7 +376,7 @@
                     )
                     return inner
 
-                lax.fori_loop(0, tiles, combine, 0)
+                lax.fori_loop(0, tiles, combine, 0, unroll=True)
                 term_copy(m, j).start()
 
             return carry
@@ -400,10 +404,11 @@
 
         def combine(i, inner):
             cols = columns_of(i)
-            total_v[:, cols] = picked(m, expert, pick, cols)
+            both = picked(m, expert, pick, cols)
+            total_v[:, cols] = both[:rows] + both[rows:]
             return inner
 
-        lax.fori_loop(0, tiles, combine, 0)
+        lax.fori_loop(0, tiles, combine, 0, unroll=True)
 
         def join(p, carry):
             @pl.when(p != pair)
@@ -415,7 +420,7 @@
                     total_v[:, cols] += terms_v[m, p, :, cols].astype(jnp.float32)
                     return inner
 
-                lax.fori_loop(0, tiles, add, 0)
+                lax.fori_loop(0, tiles, add, 0, unroll=True)
 
             return carry
 
@@ -639,7 +644,7 @@
             pltpu.VMEM((rows, width), jnp.float32),
             pltpu.VMEM((rows, experts), jnp.bfloat16),
             pltpu.VMEM((n_pairs, micro, 2 * rows, columns), jnp.bfloat16),
-            pltpu.VMEM((n_expert, micro, 2 * rows, columns), jnp.bfloat16),
+            pltpu.VMEM((n_expert, micro, rows, columns), jnp.bfloat16),
             pltpu.VMEM((micro, rows, experts), jnp.float32),
             pltpu.VMEM((micro, 2, rows, experts), jnp.float32),
             pltpu.VMEM((chunks, experts, chunk), jnp.float32),

time: 128 us -> 116 us (0.906)
  Pallas kernels: 122 us -> 110 us
    pallas_call x1, Pallas kernels: 122 us -> 110 us  [on_device(): pl.pallas_call(functools.partial(kernel, sizes), out_shape=(jax.ShapeDtyp...]
where the time goes in v3:
time: 116 us
  Pallas kernels  110 us (95%)
  local copies, waits for them, and re-layouts  4.8 us (4%)
    pallas_call x1, Pallas kernels, on_device(): pl.pallas_call(functools.partial(kernel, sizes), out_shape=(jax.ShapeDtyp...  110 us
    unnamed x5, local copies, waits for them, and re-layouts  4.8 us

profile of v3, /device:TPU:0, one launch (start us, length us, event | category | flops | bytes accessed | tf_op | source)
XLA Modules:
  0.0 115.9 jit_solution(10075860862219339932)
XLA Ops:
  0.6 1.4 %copy.8 = s32[1,4,48,2]{3,2,1,0:T(8,128)} copy(s32[1,4,48,2]{2,3,1,0:T(2,128)} %param.9) | data formatting | bytes 3072 | tf_op args[3]
  2.1 110.4 %relay.1 = (bf16[4,48,4096]{2,1,0:T(8,128)(2,1)}, f32[8,4,512]{2,1,0:T(4,128)}) custom-call(bf16[4,36,4,4096]{3,2,1,0:T(4,128)(2,1)} %bitcast.13, bf16[4,48,4096]{2,1,0:T(8,128)(2,1)} %bitcast.16, bf16[4,48,2,4096]{3,2,1,0:T(2,128)(2,1)} %bitcast.14, bf16[4,48,4096]{2,1,0:T(8,128)(2,1)} %upstream_ref.1, s32[4,48,2]{2,1,0:T(8,128)} %bitcast.17, ...), custom_call_target="tpu_custom_call" | custom-call | tf_op jit(solution)/shard_map/relay/pallas_call | solution.py:624
  112.5 0.0 copy-start
  112.5 2.7 %copy.11 = bf16[1,4,48,4096]{3,2,1,0:T(8,128)(2,1)} copy(bf16[1,4,48,4096]{3,2,1,0:T(8,128)(2,1)} %bitcast.15) | data formatting | bytes 3145728
  115.2 0.0 copy-done
  115.2 0.6 copy.12
Async XLA Ops:
  112.5 2.7 %copy-start = (f32[8,4,512]{2,1,0:T(4,128)S(1)}, f32[8,4,512]{2,1,0:T(4,128)}, u32[]{:S(2)}) copy-start(f32[8,4,512]{2,1,0:T(4,128)} %get-tuple-element.5) | copy-start | bytes 196612

commit v4 on v3

--- a/solution.py
+++ b/solution.py
@@ -32,6 +32,7 @@
     pairs_v,
     saved_v,
     inc_v,
+    out_v,
     total_v,
     dense_v,
     pick_v,
@@ -53,6 +54,7 @@
     top_sem,
     relay_send,
     relay_recv,
+    out_sem,
     part_send,
     part_recv,
     sum_send,
@@ -115,11 +117,6 @@
     def _():
         top_load.start()
 
-    pl.semaphore_wait(
-        barrier,
-        group - 1 + jnp.where(pipe > 0, 1, 0) + jnp.where(pipe < n_pipe - 1, 1, 0),
-    )
-
     def tail_copy(j):
         return pltpu.make_async_remote_copy(
             src_ref=tail_v.at[j],
@@ -235,18 +232,29 @@
 
         @pl.when(send)
         def _():
-            if rest:
-                tail_copy(j).start()
-            if whole_rows:
-                main_copy(0, j).start()
-
-    for m in range(micro):
+            main_copy(0, j).start()
+
+    def send_first_tail(t):
+        j, send = far(t)
+
+        @pl.when(send)
+        def _():
+            tail_copy(j).start()
+
+    grads_load(0).wait()
+    if whole_rows:
+        regroup_main(0)
+    pl.semaphore_wait(
+        barrier,
+        group - 1 + jnp.where(pipe > 0, 1, 0) + jnp.where(pipe < n_pipe - 1, 1, 0),
+    )
+    if whole_rows:
+        send_first(0)
+    for m in range(1, micro):
         grads_load(m).wait()
     if rest:
         lax.fori_loop(0, tiles, regroup_tail, 0, unroll=4)
-    if whole_rows:
-        regroup_main(0)
-    send_first(0)
+        send_first_tail(0)
 
     wpart_v[...] = jnp.zeros_like(wpart_v)
     for load in loads:
@@ -257,6 +265,9 @@
         lax.broadcasted_iota(jnp.int32, (rows, rows), 0)
         > lax.broadcasted_iota(jnp.int32, (rows, rows), 1)
     ).astype(jnp.bfloat16)
+    same = lax.broadcasted_iota(jnp.int32, (rows, rows), 0) == lax.broadcasted_iota(
+        jnp.int32, (rows, rows), 1
+    )
     expert_ids = lax.broadcasted_iota(jnp.int32, (rows, experts), 1)
 
     def regroup(i, carry):
@@ -271,9 +282,12 @@
         expl = jnp.exp(logits)
         probs = expl / jnp.sum(expl, axis=-1, keepdims=True)
         probs_v[m] = probs
-        named = routes_ref[m]
-        first = (named[:, 0:1] == expert_ids).astype(jnp.float32)
-        second = (named[:, 1:2] == expert_ids).astype(jnp.float32)
+        named = [
+            jnp.sum(jnp.where(same, routes_ref[m, k : k + 1, :], 0), axis=1, keepdims=True)
+            for k in range(2)
+        ]
+        first = (named[0] == expert_ids).astype(jnp.float32)
+        second = (named[1] == expert_ids).astype(jnp.float32)
         chosen_v[m, 0] = first
         chosen_v[m, 1] = second
         either = first + second
@@ -305,7 +319,10 @@
             pick_copy(p).start()
 
     for t in range(1, n_expert):
-        send_first(t)
+        if whole_rows:
+            send_first(t)
+        if rest:
+            send_first_tail(t)
 
     def send_near(m):
         if rest and m == 0:
@@ -331,6 +348,12 @@
     @pl.when(pipe == n_pipe - 1)
     def _():
         top_load.wait()
+
+    def out_copy(m, q):
+        part = pl.ds(pl.multiple_of(q * PACK, PACK), PACK)
+        return pltpu.make_async_copy(
+            out_v.at[m, part], out_ref.at[m, part], out_sem.at[m, q]
+        )
 
     def await_slots(m, j):
         if whole_rows:
@@ -390,7 +413,7 @@
     def relay(m, q):
         part = pl.ds(pl.multiple_of(q * PACK, PACK), PACK)
         return pltpu.make_async_remote_copy(
-            src_ref=out_ref.at[m, part],
+            src_ref=out_v.at[m, part],
             dst_ref=inc_v.at[m, part],
             send_sem=relay_send.at[m, q],
             recv_sem=relay_recv.at[m, q],
@@ -451,7 +474,7 @@
                 cols = pl.ds(pl.multiple_of(i * tile, tile), tile)
                 term = jnp.dot(dense, weight_ref[:, cols], preferred_element_type=jnp.float32)
                 whole = inc_v[m, part, cols].astype(jnp.float32) + total_v[part, cols] + term
-                out_ref[m, part, cols] = whole.astype(jnp.bfloat16)
+                out_v[m, part, cols] = whole.astype(jnp.bfloat16)
                 return innermost
 
             lax.fori_loop(0, width // tile, finish, 0, unroll=True)
@@ -460,6 +483,7 @@
             def _():
                 relay(m, q).start()
 
+            out_copy(m, q).start()
             return inner
 
         lax.fori_loop(0, rows // PACK, step, 0)
@@ -475,7 +499,7 @@
             )
             return inner
 
-        lax.fori_loop(0, chunks, weigh, 0)
+        lax.fori_loop(0, chunks, weigh, 0, unroll=8)
 
     def turn(m, carry):
         @pl.when(m < micro)
@@ -574,6 +598,10 @@
         def _():
             for m in range(max(micro - 2, 0), micro):
                 term_copy(m, j).wait_send()
+
+    for m in range(micro):
+        for q in range(rows // PACK):
+            out_copy(m, q).wait()
 
     for p in range(n_pairs):
 
@@ -628,7 +656,7 @@
             jax.ShapeDtypeStruct((chunks, experts, chunk), jnp.float32),
         ),
         in_specs=[any_space] * 4 + [vmem] * 2,
-        out_specs=(vmem, vmem),
+        out_specs=(any_space, vmem),
         scratch_shapes=[
             pltpu.VMEM((micro, capacity, n_expert, width), jnp.bfloat16),
             pltpu.VMEM(main_shape, jnp.bfloat16),
@@ -640,6 +668,7 @@
             pltpu.VMEM((micro, rows, width), jnp.bfloat16),
             pltpu.VMEM((micro, rows, 2, width), jnp.bfloat16),
             pltpu.VMEM((micro, 2 * rows, width), jnp.bfloat16),
+            pltpu.VMEM((micro, rows, width), jnp.bfloat16),
             pltpu.VMEM((micro, rows, width), jnp.bfloat16),
             pltpu.VMEM((rows, width), jnp.float32),
             pltpu.VMEM((rows, experts), jnp.bfloat16),
@@ -662,6 +691,7 @@
             dma,
             dma((micro, rows // PACK)),
             dma((micro, rows // PACK)),
+            dma((micro, rows // PACK)),
             dma((group,)),
             dma((group,)),
             dma((group,)),
@@ -676,7 +706,7 @@
         normed[0],
         saved_out[0],
         upstream,
-        routes[0],
+        jnp.swapaxes(routes[0], 1, 2),
         router_weight[0].T,
     )
     router_grad = jnp.transpose(wgrad, (0, 2, 1)).reshape(width, experts)

time: 116 us -> 111 us (0.957)
  Pallas kernels: 110 us -> 107 us
  local copies, waits for them, and re-layouts: 4.8 us -> 3.37 us
    pallas_call x1, Pallas kernels: 110 us -> 107 us  [on_device(): pl.pallas_call(functools.partial(kernel, sizes), out_shape=(jax.ShapeDtyp...]
    unnamed x5 -> x4, local copies, waits for them, and re-layouts: 4.8 us -> 3.37 us
where the time goes in v4:
time: 111 us
  Pallas kernels  107 us (96%)
  local copies, waits for them, and re-layouts  3.37 us (3%)
    pallas_call x1, Pallas kernels, on_device(): pl.pallas_call(functools.partial(kernel, sizes), out_shape=(jax.ShapeDtyp...  107 us
    unnamed x4, local copies, waits for them, and re-layouts  3.37 us

profile of v4, /device:TPU:0, one launch (start us, length us, event | category | flops | bytes accessed | tf_op | source)
XLA Modules:
  0.0 110.8 jit_solution(2726584282791638623)
XLA Ops:
  0.6 106.8 %relay.1 = (bf16[4,48,4096]{2,1,0:T(8,128)(2,1)}, f32[8,4,512]{2,1,0:T(4,128)}) custom-call(bf16[4,36,4,4096]{3,2,1,0:T(4,128)(2,1)} %bitcast.15, bf16[4,48,4096]{2,1,0:T(8,128)(2,1)} %bitcast.17, bf16[4,48,2,4096]{3,2,1,0:T(2,128)(2,1)} %bitcast.16, bf16[4,48,4096]{2,1,0:T(8,128)(2,1)} %upstream_ref.1, s32[4,2,48]{2,1,0:T(2,128)} %bitcast.21, ...), custom_call_target="tpu_custom_call" | custom-call | tf_op jit(solution)/shard_map/relay/pallas_call | solution.py:652
  107.5 0.0 copy-start
  107.5 2.7 %copy.10 = bf16[1,4,48,4096]{3,2,1,0:T(8,128)(2,1)} copy(bf16[1,4,48,4096]{3,2,1,0:T(8,128)(2,1)} %bitcast.18) | data formatting | bytes 3145728
  110.2 0.0 copy-done
  110.2 0.6 copy.11
Async XLA Ops:
  107.5 2.7 %copy-start = (f32[8,4,512]{2,1,0:T(4,128)S(1)}, f32[8,4,512]{2,1,0:T(4,128)}, u32[]{:S(2)}) copy-start(f32[8,4,512]{2,1,0:T(4,128)} %get-tuple-element.5) | copy-start | bytes 196612

commit v5 on v4

--- a/solution.py
+++ b/solution.py
@@ -21,6 +21,8 @@
     weight_ref,
     out_ref,
     wgrad_ref,
+    routes_v,
+    weight_v,
     grads_v,
     main_v,
     tail_v,
@@ -108,6 +110,8 @@
     loads = [
         pltpu.make_async_copy(normed_ref, normed_v, load_sem.at[0]),
         pltpu.make_async_copy(saved_ref, pairs_v, load_sem.at[1]),
+        pltpu.make_async_copy(routes_ref, routes_v, load_sem.at[2]),
+        pltpu.make_async_copy(weight_ref, weight_v, load_sem.at[3]),
     ]
     top_load = pltpu.make_async_copy(upstream_ref, inc_v, top_sem)
     for load in loads:
@@ -260,7 +264,7 @@
     for load in loads:
         load.wait()
 
-    weight = weight_ref[...]
+    weight = weight_v[...]
     earlier = (
         lax.broadcasted_iota(jnp.int32, (rows, rows), 0)
         > lax.broadcasted_iota(jnp.int32, (rows, rows), 1)
@@ -283,7 +287,7 @@
         probs = expl / jnp.sum(expl, axis=-1, keepdims=True)
         probs_v[m] = probs
         named = [
-            jnp.sum(jnp.where(same, routes_ref[m, k : k + 1, :], 0), axis=1, keepdims=True)
+            jnp.sum(jnp.where(same, routes_v[m, k : k + 1, :], 0), axis=1, keepdims=True)
             for k in range(2)
         ]
         first = (named[0] == expert_ids).astype(jnp.float32)
@@ -472,7 +476,7 @@
 
             def finish(i, innermost):
                 cols = pl.ds(pl.multiple_of(i * tile, tile), tile)
-                term = jnp.dot(dense, weight_ref[:, cols], preferred_element_type=jnp.float32)
+                term = jnp.dot(dense, weight_v[:, cols], preferred_element_type=jnp.float32)
                 whole = inc_v[m, part, cols].astype(jnp.float32) + total_v[part, cols] + term
                 out_v[m, part, cols] = whole.astype(jnp.bfloat16)
                 return innermost
@@ -626,6 +630,23 @@
     def _():
         for distance in range(1, group):
             sum_copy(distance).wait_send()
+
+
+def settle(out_ref, wgrad_ref, out_to, wgrad_to, sems):
+    micro = out_ref.shape[0]
+    copies = [pltpu.make_async_copy(wgrad_ref, wgrad_to, sems.at[sems.shape[0] - 1])]
+    pieces = out_ref.shape[1] // PACK
+    for i in range(micro * pieces):
+        part = pl.ds(i % pieces * PACK, PACK)
+        copies.append(
+            pltpu.make_async_copy(
+                out_ref.at[i // pieces, part], out_to.at[i // pieces, part], sems.at[i]
+            )
+        )
+    for copy in copies:
+        copy.start()
+    for copy in copies:
+        copy.wait()
 
 
 def on_device(sizes, normed, saved_out, expert_grads, routes, router_weight, upstream):
@@ -655,9 +676,11 @@
             jax.ShapeDtypeStruct((micro, rows, width), jnp.bfloat16),
             jax.ShapeDtypeStruct((chunks, experts, chunk), jnp.float32),
         ),
-        in_specs=[any_space] * 4 + [vmem] * 2,
+        in_specs=[any_space] * 6,
         out_specs=(any_space, vmem),
         scratch_shapes=[
+            pltpu.VMEM((micro, 2, rows), jnp.int32),
+            pltpu.VMEM((experts, width), jnp.bfloat16),
             pltpu.VMEM((micro, capacity, n_expert, width), jnp.bfloat16),
             pltpu.VMEM(main_shape, jnp.bfloat16),
             pltpu.VMEM(tail_shape, jnp.bfloat16),
@@ -687,7 +710,7 @@
             dma((n_expert,)),
             dma((micro, n_expert)),
             dma((micro, n_pairs)),
-            dma((2,)),
+            dma((4,)),
             dma,
             dma((micro, rows // PACK)),
             dma((micro, rows // PACK)),
@@ -709,6 +732,18 @@
         jnp.swapaxes(routes[0], 1, 2),
         router_weight[0].T,
     )
+    out, wgrad = pl.pallas_call(
+        settle,
+        out_shape=(
+            jax.ShapeDtypeStruct(out.shape, out.dtype),
+            jax.ShapeDtypeStruct(wgrad.shape, wgrad.dtype),
+        ),
+        in_specs=[any_space] * 2,
+        out_specs=(any_space, any_space),
+        scratch_shapes=[dma((micro * (rows // PACK) + 1,))],
+        compiler_params=pltpu.CompilerParams(vmem_limit_bytes=60 * 2**20),
+        name="settle",
+    )(out, wgrad)
     router_grad = jnp.transpose(wgrad, (0, 2, 1)).reshape(width, experts)
     return (out[None], router_grad[None])
 

time: 111 us -> 158 us (1.42)
  Pallas kernels: 107 us -> 157 us
  local copies, waits for them, and re-layouts: 3.37 us -> 0 us
    pallas_call x0 -> x1, Pallas kernels: none -> 50.9 us  [on_device(): pl.pallas_call(settle, out_shape=(jax.ShapeDtypeStruct(out.shape, out.dty...]
    unnamed x4 -> x0, local copies, waits for them, and re-layouts: 3.37 us -> none
where the time goes in v5:
time: 158 us
  Pallas kernels  157 us (99%)
    pallas_call x1, Pallas kernels, on_device(): pl.pallas_call(functools.partial(kernel, sizes), out_shape=(jax.ShapeDtyp...  106 us
    pallas_call x1, Pallas kernels, on_device(): pl.pallas_call(settle, out_shape=(jax.ShapeDtypeStruct(out.shape, out.dty...  50.9 us

profile of v5, /device:TPU:0, one launch (start us, length us, event | category | flops | bytes accessed | tf_op | source)
XLA Modules:
  0.0 157.7 jit_solution(7919537483587736448)
XLA Ops:
  0.6 106.2 %relay.1 = (bf16[4,48,4096]{2,1,0:T(8,128)(2,1)}, f32[8,4,512]{2,1,0:T(4,128)}) custom-call(bf16[4,36,4,4096]{3,2,1,0:T(4,128)(2,1)} %bitcast.15, bf16[4,48,4096]{2,1,0:T(8,128)(2,1)} %bitcast.17, bf16[4,48,2,4096]{3,2,1,0:T(2,128)(2,1)} %bitcast.16, bf16[4,48,4096]{2,1,0:T(8,128)(2,1)} %upstream_ref.1, s32[4,2,48]{2,1,0:T(2,128)} %bitcast.19, ...), custom_call_target="tpu_custom_call" | custom-call | tf_op jit(solution)/shard_map/relay/pallas_call | solution.py:673
  106.8 50.9 %settle.1 = (bf16[4,48,4096]{2,1,0:T(8,128)(2,1)}, f32[8,4,512]{2,1,0:T(4,128)}) custom-call(bf16[4,48,4096]{2,1,0:T(8,128)(2,1)} %get-tuple-element.6.out_ref, f32[8,4,512]{2,1,0:T(4,128)} %get-tuple-element.7.wgrad_ref), custom_call_target="tpu_custom_call" | custom-call | tf_op jit(solution)/shard_map/settle/pallas_call | solution.py:735

commit v6 on v5

--- a/solution.py
+++ b/solution.py
@@ -105,8 +105,7 @@
     def grads_load(m):
         return pltpu.make_async_copy(grads_ref.at[m], grads_v.at[m], grads_sem.at[m])
 
-    for m in range(micro):
-        grads_load(m).start()
+    grads_load(0).start()
     loads = [
         pltpu.make_async_copy(normed_ref, normed_v, load_sem.at[0]),
         pltpu.make_async_copy(saved_ref, pairs_v, load_sem.at[1]),
@@ -114,13 +113,6 @@
         pltpu.make_async_copy(weight_ref, weight_v, load_sem.at[3]),
     ]
     top_load = pltpu.make_async_copy(upstream_ref, inc_v, top_sem)
-    for load in loads:
-        load.start()
-
-    @pl.when(pipe == n_pipe - 1)
-    def _():
-        top_load.start()
-
     def tail_copy(j):
         return pltpu.make_async_remote_copy(
             src_ref=tail_v.at[j],
@@ -246,6 +238,15 @@
             tail_copy(j).start()
 
     grads_load(0).wait()
+    for m in range(1, micro):
+        grads_load(m).start()
+    for load in loads:
+        load.start()
+
+    @pl.when(pipe == n_pipe - 1)
+    def _():
+        top_load.start()
+
     if whole_rows:
         regroup_main(0)
     pl.semaphore_wait(
@@ -632,21 +633,22 @@
             sum_copy(distance).wait_send()
 
 
-def settle(out_ref, wgrad_ref, out_to, wgrad_to, sems):
+def settle(out_ref, wgrad_ref, out_to, wgrad_to, out_v, wgrad_v, load_sems, store_sems):
     micro = out_ref.shape[0]
-    copies = [pltpu.make_async_copy(wgrad_ref, wgrad_to, sems.at[sems.shape[0] - 1])]
-    pieces = out_ref.shape[1] // PACK
-    for i in range(micro * pieces):
-        part = pl.ds(i % pieces * PACK, PACK)
-        copies.append(
-            pltpu.make_async_copy(
-                out_ref.at[i // pieces, part], out_to.at[i // pieces, part], sems.at[i]
-            )
-        )
-    for copy in copies:
-        copy.start()
-    for copy in copies:
-        copy.wait()
+    ways = [(wgrad_ref, wgrad_v, wgrad_to)]
+    for m in range(micro):
+        ways.append((out_ref.at[m], out_v.at[m], out_to.at[m]))
+    loads, stores = [], []
+    for i, (source, held, target) in enumerate(ways):
+        loads.append(pltpu.make_async_copy(source, held, load_sems.at[i]))
+        stores.append(pltpu.make_async_copy(held, target, store_sems.at[i]))
+    for load in loads:
+        load.start()
+    for load, store in zip(loads, stores):
+        load.wait()
+        store.start()
+    for store in stores:
+        store.wait()
 
 
 def on_device(sizes, normed, saved_out, expert_grads, routes, router_weight, upstream):
@@ -740,7 +742,12 @@
         ),
         in_specs=[any_space] * 2,
         out_specs=(any_space, any_space),
-        scratch_shapes=[dma((micro * (rows // PACK) + 1,))],
+        scratch_shapes=[
+            pltpu.VMEM(out.shape, out.dtype),
+            pltpu.VMEM(wgrad.shape, wgrad.dtype),
+            dma((micro + 1,)),
+            dma((micro + 1,)),
+        ],
         compiler_params=pltpu.CompilerParams(vmem_limit_bytes=60 * 2**20),
         name="settle",
     )(out, wgrad)

time: 158 us -> 109 us (0.69)
  Pallas kernels: 157 us -> 108 us
    pallas_call x1, Pallas kernels: 50.9 us -> 2.25 us  [on_device(): pl.pallas_call(settle, out_shape=(jax.ShapeDtypeStruct(out.shape, out.dty...]
where the time goes in v6:
time: 109 us
  Pallas kernels  108 us (99%)
    pallas_call x1, Pallas kernels, on_device(): pl.pallas_call(functools.partial(kernel, sizes), out_shape=(jax.ShapeDtyp...  106 us
    pallas_call x1, Pallas kernels, on_device(): pl.pallas_call(settle, out_shape=(jax.ShapeDtypeStruct(out.shape, out.dty...  2.25 us

profile of v6, /device:TPU:0, one launch (start us, length us, event | category | flops | bytes accessed | tf_op | source)
XLA Modules:
  0.0 109.1 jit_solution(15107569886563327545)
XLA Ops:
  0.6 106.2 %relay.1 = (bf16[4,48,4096]{2,1,0:T(8,128)(2,1)}, f32[8,4,512]{2,1,0:T(4,128)}) custom-call(bf16[4,36,4,4096]{3,2,1,0:T(4,128)(2,1)} %bitcast.15, bf16[4,48,4096]{2,1,0:T(8,128)(2,1)} %bitcast.17, bf16[4,48,2,4096]{3,2,1,0:T(2,128)(2,1)} %bitcast.16, bf16[4,48,4096]{2,1,0:T(8,128)(2,1)} %upstream_ref.1, s32[4,2,48]{2,1,0:T(2,128)} %bitcast.19, ...), custom_call_target="tpu_custom_call" | custom-call | tf_op jit(solution)/shard_map/relay/pallas_call | solution.py:675
  106.8 2.3 %settle.1 = (bf16[4,48,4096]{2,1,0:T(8,128)(2,1)}, f32[8,4,512]{2,1,0:T(4,128)}) custom-call(bf16[4,48,4096]{2,1,0:T(8,128)(2,1)} %get-tuple-element.6.out_ref, f32[8,4,512]{2,1,0:T(4,128)} %get-tuple-element.7.wgrad_ref), custom_call_target="tpu_custom_call" | custom-call | tf_op jit(solution)/shard_map/settle/pallas_call | solution.py:737

commit v7 on v6

--- a/solution.py
+++ b/solution.py
@@ -491,7 +491,7 @@
             out_copy(m, q).start()
             return inner
 
-        lax.fori_loop(0, rows // PACK, step, 0)
+        lax.fori_loop(0, rows // PACK, step, 0, unroll=True)
         dense = dense_v[...]
 
         def weigh(i, inner):

time: 109 us -> 109 us (level)
  no operation moved by 1% of the time
where the time goes in v7:
time: 109 us
  Pallas kernels  108 us (99%)
    pallas_call x1, Pallas kernels, on_device(): pl.pallas_call(functools.partial(kernel, sizes), out_shape=(jax.ShapeDtyp...  106 us
    pallas_call x1, Pallas kernels, on_device(): pl.pallas_call(settle, out_shape=(jax.ShapeDtypeStruct(out.shape, out.dty...  2.25 us

profile of v7, /device:TPU:0, one launch (start us, length us, event | category | flops | bytes accessed | tf_op | source)
XLA Modules:
  0.0 109.1 jit_solution(13023478703689522841)
XLA Ops:
  0.6 106.2 %relay.1 = (bf16[4,48,4096]{2,1,0:T(8,128)(2,1)}, f32[8,4,512]{2,1,0:T(4,128)}) custom-call(bf16[4,36,4,4096]{3,2,1,0:T(4,128)(2,1)} %bitcast.15, bf16[4,48,4096]{2,1,0:T(8,128)(2,1)} %bitcast.17, bf16[4,48,2,4096]{3,2,1,0:T(2,128)(2,1)} %bitcast.16, bf16[4,48,4096]{2,1,0:T(8,128)(2,1)} %upstream_ref.1, s32[4,2,48]{2,1,0:T(2,128)} %bitcast.19, ...), custom_call_target="tpu_custom_call" | custom-call | tf_op jit(solution)/shard_map/relay/pallas_call | solution.py:675
  106.8 2.3 %settle.1 = (bf16[4,48,4096]{2,1,0:T(8,128)(2,1)}, f32[8,4,512]{2,1,0:T(4,128)}) custom-call(bf16[4,48,4096]{2,1,0:T(8,128)(2,1)} %get-tuple-element.6.out_ref, f32[8,4,512]{2,1,0:T(4,128)} %get-tuple-element.7.wgrad_ref), custom_call_target="tpu_custom_call" | custom-call | tf_op jit(solution)/shard_map/settle/pallas_call | solution.py:737
